TPU v7x, 32 devices: a whole 2x2x4 slice. The times are simulated.
32 devices in a mesh: frame: 8 (over z, core), video: 4 (over y, x).
Axes of the slice: x: 2, y: 2, z: 4, core: 2. Of those that a mesh axis runs over, the one named last changes fastest.
Arguments:
- video: bfloat16 [24, 8, 197, 768], P('video', 'frame'), may hold values from -6 to 6
- video_live: int32 [24], P('video'), may hold values 0 or 1
- cotangent: bfloat16 [24, 8, 198, 768], P('video', 'frame'), may hold values from -6 to 6
- message_proj: bfloat16 [768, 768], replicated, may hold values from -0.21875 to 0.21875
- message_bias: float32 [768], replicated, may hold values from -3 to 3
- message_gain: float32 [768], replicated, may hold values from 0.5 to 1.5
- message_shift: float32 [768], replicated, may hold values from -1.75 to 1.75
- message_qkv: bfloat16 [768, 2304], replicated, may hold values from -0.21875 to 0.21875
- message_out: bfloat16 [768, 768], replicated, may hold values from -0.4375 to 0.4375
- frame_gain: float32 [768], replicated, may hold values from 0.5 to 1.5
- frame_shift: float32 [768], replicated, may hold values from -1.75 to 1.75
- frame_qkv: bfloat16 [768, 2304], replicated, may hold values from -0.21875 to 0.21875
- frame_out: bfloat16 [768, 768], replicated, may hold values from -0.875 to 0.875
- dense_gain: float32 [768], replicated, may hold values from 0.5 to 1.5
- dense_shift: float32 [768], replicated, may hold values from -1.75 to 1.75
- dense_in: bfloat16 [768, 3072], replicated, may hold values from -0.21875 to 0.21875
- dense_in_bias: float32 [3072], replicated, may hold values from -3 to 3
- dense_out: bfloat16 [3072, 768], replicated, may hold values from -0.21875 to 0.21875
- dense_out_bias: float32 [768], replicated, may hold values from -3 to 3
Outputs:
- output: bfloat16 [24, 8, 198, 768], P('video', 'frame')
- grad_video: bfloat16 [24, 8, 197, 768], P('video', 'frame')
- grad_message_proj: float32 [768, 768], P('video')
- grad_message_bias: float32 [768], P('video')
- grad_message_gain: float32 [768], P('video')
- grad_message_shift: float32 [768], P('video')
- grad_message_qkv: float32 [768, 2304], P('video')
- grad_message_out: float32 [768, 768], P('video')
- grad_frame_gain: float32 [768], P('video')
- grad_frame_shift: float32 [768], P('video')
- grad_frame_qkv: float32 [768, 2304], P('video')
- grad_frame_out: float32 [768, 768], P('video')
- grad_dense_gain: float32 [768], P('video')
- grad_dense_shift: float32 [768], P('video')
- grad_dense_in: float32 [768, 3072], P('video')
- grad_dense_in_bias: float32 [3072], P('video')
- grad_dense_out: float32 [3072, 768], P('video')
- grad_dense_out_bias: float32 [768], P('video')
Inputs may be any that keep to these rules, and one draw needn't show every extreme that they name: `video_live`: 1 marks a video whose output gradient counts, 0 a padded slot.
All inputs are finite; a program needn't handle non-finite values. No bound on the sum of `video_live` on one device may be relied on, other than what follows from the above.
Results may differ from a plain program's by a relative error of at most 0.025.
Values may be sent and summed in bfloat16 or wider, within the bound.
A program may use at most 192 MiB of HBM per device.

v0:
```python
import jax
import jax.numpy as jnp
from jax import lax
from jax.sharding import PartitionSpec as P

HEADS = 12
HEAD_DIM = 64


EPS = 1e-05


def column_sum(values):
    return jnp.sum(values.reshape(-1, values.shape[-1]), axis=0)


def matmul(left, right):
    return jnp.dot(left, right, preferred_element_type=jnp.float32)


def back_matmul(grad_low, weight):
    return lax.dot_general(
        grad_low,
        weight,
        (((grad_low.ndim - 1,), (1,)), ((), ())),
        preferred_element_type=jnp.float32,
    )


def weight_grad(inputs_low, grad_low):
    left = inputs_low.reshape(-1, inputs_low.shape[-1])
    right = grad_low.reshape(-1, grad_low.shape[-1])
    return lax.dot_general(
        left, right, (((0,), (0,)), ((), ())), preferred_element_type=jnp.float32
    )


def norm_forward(values, gain, shift):
    center = values - jnp.mean(values, axis=-1, keepdims=True)
    inverse = lax.rsqrt(jnp.mean(center * center, axis=-1, keepdims=True) + EPS)
    scaled = center * inverse
    return (scaled * gain + shift, scaled, inverse)


def norm_backward(grad_out, scaled, inverse, gain):
    grad_scaled = grad_out * gain
    grad_in = inverse * (
        grad_scaled
        - jnp.mean(grad_scaled, axis=-1, keepdims=True)
        - scaled * jnp.mean(grad_scaled * scaled, axis=-1, keepdims=True)
    )
    return (grad_in, column_sum(grad_out * scaled), column_sum(grad_out))


def split_heads(values):
    return values.reshape(values.shape[:-1] + (HEADS, HEAD_DIM))


def attend_forward(query_rows, key_rows, value_rows):
    scores = (
        jnp.einsum("bqhd,bkhd->bhqk", query_rows, key_rows, preferred_element_type=jnp.float32)
        * 0.125
    )
    largest = jnp.max(scores, axis=-1, keepdims=True)
    raised = jnp.exp(scores - largest)
    total = jnp.sum(raised, axis=-1, keepdims=True)
    probs_low = (raised / total).astype(jnp.bfloat16)
    mixed = jnp.einsum("bhqk,bkhd->bqhd", probs_low, value_rows, preferred_element_type=jnp.float32)
    return (mixed, largest + jnp.log(total))


def attend_backward(query_rows, key_rows, value_rows, log_total, grad_mixed):
    scores = (
        jnp.einsum("bqhd,bkhd->bhqk", query_rows, key_rows, preferred_element_type=jnp.float32)
        * 0.125
    )
    probs = jnp.exp(scores - log_total)
    grad_probs = jnp.einsum(
        "bqhd,bkhd->bhqk", grad_mixed, value_rows, preferred_element_type=jnp.float32
    )
    grad_scores = probs * (grad_probs - jnp.sum(grad_probs * probs, axis=-1, keepdims=True))
    grad_low = grad_scores.astype(jnp.bfloat16)
    grad_query = (
        jnp.einsum("bhqk,bkhd->bqhd", grad_low, key_rows, preferred_element_type=jnp.float32)
        * 0.125
    )
    grad_key = (
        jnp.einsum("bhqk,bqhd->bkhd", grad_low, query_rows, preferred_element_type=jnp.float32)
        * 0.125
    )
    grad_value = jnp.einsum(
        "bhqk,bqhd->bkhd",
        probs.astype(jnp.bfloat16),
        grad_mixed,
        preferred_element_type=jnp.float32,
    )
    return (grad_query, grad_key, grad_value)


def local(
    video,
    video_live,
    cotangent,
    message_proj,
    message_bias,
    message_gain,
    message_shift,
    message_qkv,
    message_out,
    frame_gain,
    frame_shift,
    frame_qkv,
    frame_out,
    dense_gain,
    dense_shift,
    dense_in,
    dense_in_bias,
    dense_out,
    dense_out_bias,
):
    width = video.shape[-1]
    batch = video.shape[0]
    frames_local = video.shape[1]
    patches = video.shape[2]
    frames_all = frames_local * lax.axis_size("frame")
    class_rows = video[:, :, 0, :]
    message = (matmul(class_rows, message_proj) + message_bias).astype(jnp.bfloat16)
    message_wide = message.astype(jnp.float32)
    normed_own, scaled_own, inverse_own = norm_forward(message_wide, message_gain, message_shift)
    normed_low = normed_own.astype(jnp.bfloat16)
    everyone = lax.all_gather(message, "frame", axis=1, tiled=True)
    normed_all = norm_forward(everyone.astype(jnp.float32), message_gain, message_shift)[0]
    key_value = matmul(normed_all.astype(jnp.bfloat16), message_qkv[:, width:]).astype(jnp.bfloat16)
    query_own = matmul(normed_low, message_qkv[:, :width]).astype(jnp.bfloat16)
    message_query = split_heads(query_own)
    message_key = split_heads(key_value[..., :width])
    message_value = split_heads(key_value[..., width:])
    message_mixed, message_total = attend_forward(message_query, message_key, message_value)
    message_mixed_low = message_mixed.reshape(batch, frames_local, width).astype(jnp.bfloat16)
    message_next = message_wide + matmul(message_mixed_low, message_out)
    tokens = jnp.concatenate([video.astype(jnp.float32), message_next[:, :, None, :]], axis=2)
    count = tokens.shape[2]
    frames_flat = batch * frames_local
    tokens = tokens.reshape(frames_flat, count, width)
    normed_first, scaled_first, inverse_first = norm_forward(tokens, frame_gain, frame_shift)
    first_low = normed_first.astype(jnp.bfloat16)
    packed_frame = matmul(first_low, frame_qkv).astype(jnp.bfloat16)
    frame_query = split_heads(packed_frame[..., :width])
    frame_key = split_heads(packed_frame[..., width : 2 * width])
    frame_value = split_heads(packed_frame[..., 2 * width :])
    frame_mixed, frame_total = attend_forward(frame_query, frame_key, frame_value)
    frame_mixed_low = frame_mixed.reshape(frames_flat, count, width).astype(jnp.bfloat16)
    middle = tokens + matmul(frame_mixed_low, frame_out)
    normed_second, scaled_second, inverse_second = norm_forward(middle, dense_gain, dense_shift)
    second_low = normed_second.astype(jnp.bfloat16)
    inner = matmul(second_low, dense_in) + dense_in_bias
    gate_sig = jax.nn.sigmoid(1.702 * inner)
    active_low = (inner * gate_sig).astype(jnp.bfloat16)
    output = middle + matmul(active_low, dense_out) + dense_out_bias
    result = output.reshape(batch, frames_local, count, width).astype(jnp.bfloat16)
    live_weight = video_live.astype(jnp.float32)[:, None, None, None]
    grad_out = (cotangent.astype(jnp.float32) * live_weight).reshape(frames_flat, count, width)
    grad_dense_out_bias = column_sum(grad_out)
    grad_out_low = grad_out.astype(jnp.bfloat16)
    grad_dense_out = weight_grad(active_low, grad_out_low)
    grad_active = back_matmul(grad_out_low, dense_out)
    grad_inner = grad_active * (gate_sig + 1.702 * inner * gate_sig * (1.0 - gate_sig))
    grad_dense_in_bias = column_sum(grad_inner)
    grad_inner_low = grad_inner.astype(jnp.bfloat16)
    grad_dense_in = weight_grad(second_low, grad_inner_low)
    grad_second, grad_dense_gain, grad_dense_shift = norm_backward(
        back_matmul(grad_inner_low, dense_in), scaled_second, inverse_second, dense_gain
    )
    grad_middle = grad_out + grad_second
    grad_middle_low = grad_middle.astype(jnp.bfloat16)
    grad_frame_out = weight_grad(frame_mixed_low, grad_middle_low)
    grad_frame_mixed = split_heads(back_matmul(grad_middle_low, frame_out).astype(jnp.bfloat16))
    grad_fq, grad_fk, grad_fv = attend_backward(
        frame_query, frame_key, frame_value, frame_total, grad_frame_mixed
    )
    grad_packed = jnp.concatenate(
        [
            grad_fq.reshape(frames_flat, count, width),
            grad_fk.reshape(frames_flat, count, width),
            grad_fv.reshape(frames_flat, count, width),
        ],
        axis=-1,
    ).astype(jnp.bfloat16)
    grad_frame_qkv = weight_grad(first_low, grad_packed)
    grad_first, grad_frame_gain, grad_frame_shift = norm_backward(
        back_matmul(grad_packed, frame_qkv), scaled_first, inverse_first, frame_gain
    )
    grad_tokens = (grad_middle + grad_first).reshape(batch, frames_local, count, width)
    grad_patches = grad_tokens[:, :, :patches]
    grad_next = grad_tokens[:, :, patches]
    grad_next_low = grad_next.astype(jnp.bfloat16)
    grad_message_out = weight_grad(message_mixed_low, grad_next_low)
    grad_message_mixed = split_heads(back_matmul(grad_next_low, message_out).astype(jnp.bfloat16))
    grad_mq, grad_mk, grad_mv = attend_backward(
        message_query, message_key, message_value, message_total, grad_message_mixed
    )
    key_value_grad = jnp.concatenate(
        [grad_mk.reshape(batch, frames_all, width), grad_mv.reshape(batch, frames_all, width)],
        axis=-1,
    )
    own_key_value = lax.psum_scatter(
        key_value_grad.astype(jnp.bfloat16), "frame", scatter_dimension=1, tiled=True
    ).astype(jnp.float32)
    grad_message_packed = jnp.concatenate(
        [grad_mq.reshape(batch, frames_local, width), own_key_value], axis=-1
    ).astype(jnp.bfloat16)
    grad_message_qkv = weight_grad(normed_low, grad_message_packed)
    grad_norm_in, grad_message_gain, grad_message_shift = norm_backward(
        back_matmul(grad_message_packed, message_qkv), scaled_own, inverse_own, message_gain
    )
    grad_message = grad_next + grad_norm_in
    grad_message_bias = column_sum(grad_message)
    grad_message_low = grad_message.astype(jnp.bfloat16)
    grad_message_proj = weight_grad(class_rows, grad_message_low)
    grad_class = back_matmul(grad_message_low, message_proj)
    grad_input = jnp.concatenate(
        [grad_patches[:, :, :1] + grad_class[:, :, None, :], grad_patches[:, :, 1:]], axis=2
    ).astype(jnp.bfloat16)
    shares = (
        lax.psum_scatter(
            grad_message_proj.astype(jnp.bfloat16), "video", scatter_dimension=0, tiled=True
        ).astype(jnp.float32),
        lax.psum_scatter(
            grad_message_bias.astype(jnp.bfloat16), "video", scatter_dimension=0, tiled=True
        ).astype(jnp.float32),
        lax.psum_scatter(
            grad_message_gain.astype(jnp.bfloat16), "video", scatter_dimension=0, tiled=True
        ).astype(jnp.float32),
        lax.psum_scatter(
            grad_message_shift.astype(jnp.bfloat16), "video", scatter_dimension=0, tiled=True
        ).astype(jnp.float32),
        lax.psum_scatter(
            grad_message_qkv.astype(jnp.bfloat16), "video", scatter_dimension=0, tiled=True
        ).astype(jnp.float32),
        lax.psum_scatter(
            grad_message_out.astype(jnp.bfloat16), "video", scatter_dimension=0, tiled=True
        ).astype(jnp.float32),
        lax.psum_scatter(
            grad_frame_gain.astype(jnp.bfloat16), "video", scatter_dimension=0, tiled=True
        ).astype(jnp.float32),
        lax.psum_scatter(
            grad_frame_shift.astype(jnp.bfloat16), "video", scatter_dimension=0, tiled=True
        ).astype(jnp.float32),
        lax.psum_scatter(
            grad_frame_qkv.astype(jnp.bfloat16), "video", scatter_dimension=0, tiled=True
        ).astype(jnp.float32),
        lax.psum_scatter(
            grad_frame_out.astype(jnp.bfloat16), "video", scatter_dimension=0, tiled=True
        ).astype(jnp.float32),
        lax.psum_scatter(
            grad_dense_gain.astype(jnp.bfloat16), "video", scatter_dimension=0, tiled=True
        ).astype(jnp.float32),
        lax.psum_scatter(
            grad_dense_shift.astype(jnp.bfloat16), "video", scatter_dimension=0, tiled=True
        ).astype(jnp.float32),
        lax.psum_scatter(
            grad_dense_in.astype(jnp.bfloat16), "video", scatter_dimension=0, tiled=True
        ).astype(jnp.float32),
        lax.psum_scatter(
            grad_dense_in_bias.astype(jnp.bfloat16), "video", scatter_dimension=0, tiled=True
        ).astype(jnp.float32),
        lax.psum_scatter(
            grad_dense_out.astype(jnp.bfloat16), "video", scatter_dimension=0, tiled=True
        ).astype(jnp.float32),
        lax.psum_scatter(
            grad_dense_out_bias.astype(jnp.bfloat16), "video", scatter_dimension=0, tiled=True
        ).astype(jnp.float32),
    )
    totals = tuple(
        (
            lax.psum(shares[0].astype(jnp.bfloat16), "frame").astype(jnp.float32),
            lax.psum(shares[1].astype(jnp.bfloat16), "frame").astype(jnp.float32),
            lax.psum(shares[2].astype(jnp.bfloat16), "frame").astype(jnp.float32),
            lax.psum(shares[3].astype(jnp.bfloat16), "frame").astype(jnp.float32),
            lax.psum(shares[4].astype(jnp.bfloat16), "frame").astype(jnp.float32),
            lax.psum(shares[5].astype(jnp.bfloat16), "frame").astype(jnp.float32),
            lax.psum(shares[6].astype(jnp.bfloat16), "frame").astype(jnp.float32),
            lax.psum(shares[7].astype(jnp.bfloat16), "frame").astype(jnp.float32),
            lax.psum(shares[8].astype(jnp.bfloat16), "frame").astype(jnp.float32),
            lax.psum(shares[9].astype(jnp.bfloat16), "frame").astype(jnp.float32),
            lax.psum(shares[10].astype(jnp.bfloat16), "frame").astype(jnp.float32),
            lax.psum(shares[11].astype(jnp.bfloat16), "frame").astype(jnp.float32),
            lax.psum(shares[12].astype(jnp.bfloat16), "frame").astype(jnp.float32),
            lax.psum(shares[13].astype(jnp.bfloat16), "frame").astype(jnp.float32),
            lax.psum(shares[14].astype(jnp.bfloat16), "frame").astype(jnp.float32),
            lax.psum(shares[15].astype(jnp.bfloat16), "frame").astype(jnp.float32),
        )
    )
    return (
        result,
        grad_input,
        totals[0],
        totals[1],
        totals[2],
        totals[3],
        totals[4],
        totals[5],
        totals[6],
        totals[7],
        totals[8],
        totals[9],
        totals[10],
        totals[11],
        totals[12],
        totals[13],
        totals[14],
        totals[15],
    )


def solution(mesh):
    in_specs = (
        P("video", "frame", None, None),
        P("video"),
        P("video", "frame", None, None),
        P(),
        P(),
        P(),
        P(),
        P(),
        P(),
        P(),
        P(),
        P(),
        P(),
        P(),
        P(),
        P(),
        P(),
        P(),
        P(),
    )
    out_specs = (
        P("video", "frame", None, None),
        P("video", "frame", None, None),
        P("video", None),
        P("video"),
        P("video"),
        P("video"),
        P("video", None),
        P("video", None),
        P("video"),
        P("video"),
        P("video", None),
        P("video", None),
        P("video"),
        P("video"),
        P("video", None),
        P("video"),
        P("video", None),
        P("video"),
    )
    return jax.shard_map(local, mesh=mesh, in_specs=in_specs, out_specs=out_specs, check_vma=False)
```

profile of v0, /device:TPU:0, one launch (start us, length us, event | category | flops | bytes accessed | tf_op | source)
XLA Modules:
  0.0 736.4 jit_solution(10615845980153967480)
XLA Ops:
  16.7 15.7 %all-gather = bf16[6,6144]{1,0:T(8,128)(2,1)S(1)} all-gather(bf16[6,768]{1,0:T(8,128)(2,1)S(1)} %get-tuple-element.173), channel_id=2, replica_groups=mesh['frame'=8,'video'=4] {'frame'}, dimensions={1}, use_global_device_ids=true | all-gather | bytes 82944 | tf_op jit(solution)/shard_map/all_gather | solution.py:131
  77.2 9.8 %multiply_reduce_fusion.1 = (f32[6,12,198]{2,1,0:T(8,128)S(1)}, f32[6,12,198,198]{2,3,1,0:T(8,128)}) fusion(bf16[6,198,12,64]{1,3,2,0:T(8,128)(2,1)} %bitcast.215, bf16[6,198,12,64]{1,3,2,0:T(8,128)(2,1)} %bitcast.211), kind=kOutput, calls=%fused_computation.10 | convolution fusion | flops 366935168 | bytes 14997312 | tf_op jit(solution)/shard_map/bqhd,bkhd->bhqk/dot_general | solution.py:61
  96.5 10.2 %fusion.28 = bf16[6,12,64,198]{3,2,1,0:T(8,128)(2,1)} fusion(bf16[6,198,12,64]{1,3,2,0:T(8,128)(2,1)S(1)} %bitcast.218, f32[6,12,198,198]{2,3,1,0:T(8,128)} %get-tuple-element.175, f32[6,12,198]{2,1,0:T(8,128)S(1)} %fusion.1, f32[6,12,198]{2,1,0:T(8,128)S(1)} %get-tuple-element.174), kind=kOutput, calls=%fused_computation.63 | convolution fusion | flops 373507200 | bytes 15054336 | tf_op jit(solution)/shard_map/bhqk,bkhd->bqhd/dot_general | solution.py:68
  111.3 11.9 %multiply_convert_fusion.1 = (bf16[6,198,3072]{2,1,0:T(8,128)(2,1)}, f32[6,198,3072]{2,1,0:T(8,128)}) fusion(f32[3072]{0:T(1024)S(1)} %copy-done.52, bf16[768,3072]{1,0:T(8,128)(2,1)S(1)} %bitcast.228, f32[6,198,768]{2,1,0:T(8,128)S(1)} %get-tuple-element.177, f32[768]{0:T(1024)S(1)} %copy-done.54, f32[768]{0:T(1024)S(1)} %copy-done.45, ...), kind=kOutput, calls=%fused_computation.5 | convolution fusion | flops 5635795968 | bytes 30293280 | tf_op jit(solution)/shard_map/dot_general | solution.py:18
  123.2 15.2 %fusion.110 = (bf16[3072]{0:T(1024)(128)(2,1)}, bf16[6,198,3072]{2,1,0:T(8,128)(2,1)}) fusion(f32[6,198,3072]{2,1,0:T(8,128)} %get-tuple-element.179, f32[3072]{0:T(1024)S(1)} %copy-done.52, bf16[3072,768]{1,0:T(8,128)(2,1)} %param.36, bf16[6,1,198,768]{3,2,1,0:T(8,128)(2,1)S(1)} %copy-done.13, f32[6]{0:T(128)S(1)} %copy-done.48), kind=kOutput, calls=%fused_computation.182 | convolution fusion | flops 5652215808 | bytes 28459032 | tf_op jit(solution)/shard_map/dot_general | solution.py:22
  138.4 9.8 %multiply_reduce_fusion.2 = (bf16[768]{0:T(1024)(128)(2,1)}, f32[6,198]{1,0:T(8,128)S(1)}, f32[6,198]{1,0:T(8,128)S(1)}, bf16[768]{0:T(1024)(128)(2,1)}, f32[6,198,768]{2,1,0:T(8,128)S(1)}) fusion(f32[6,198,768]{2,1,0:T(8,128)S(1)} %get-tuple-element.177, f32[6,198]{1,0:T(8,128)S(1)} %add_rsqrt_fusion, f32[6,198]{1,0:T(8,128)S(1)} %broadcast_multiply_fusion.4, ...), kind=kOutput, calls=%fused_computation.37 | convolution fusion | flops 5613894656 | bytes 19341888 | tf_op jit(solution)/shard_map/dot_general | solution.py:22
  158.8 10.2 %fusion.29 = bf16[6,12,64,198]{3,2,1,0:T(8,128)(2,1)} fusion(bf16[6,198,12,64]{1,3,2,0:T(8,128)(2,1)} %bitcast.213, f32[6,12,198,198]{2,3,1,0:T(8,128)} %get-tuple-element.175, f32[6,12,198]{2,1,0:T(8,128)} %log_add_fusion), kind=kOutput, calls=%fused_computation.64 | convolution fusion | flops 370684512 | bytes 14997312 | tf_op jit(solution)/shard_map/bhqk,bqhd->bkhd/dot_general | solution.py:91
  169.0 10.3 %multiply_reduce_fusion = (f32[6,12,198]{2,1,0:T(8,128)S(1)}, f32[6,12,198,198]{2,3,1,0:T(8,128)}) fusion(f32[6,12,198,198]{2,3,1,0:T(8,128)} %get-tuple-element.175, f32[6,12,198]{2,1,0:T(8,128)S(1)} %copy-done.16, bf16[6,198,12,64]{1,3,2,0:T(8,128)(2,1)S(1)} %bitcast.214, bf16[6,198,12,64]{1,3,2,0:T(8,128)(2,1)S(1)} %bitcast.219), kind=kOutput, calls=%fused_computation.2 | convolution fusion | flops 372580544 | bytes 26345088 | tf_op jit(solution)/shard_map/bqhd,bkhd->bhqk/dot_general | solution.py:78
  179.2 10.8 %multiply_convert_fusion = bf16[6,12,198,198]{2,3,1,0:T(8,128)(2,1)S(1)} fusion(f32[6,12,198,198]{2,3,1,0:T(8,128)} %get-tuple-element.182, f32[6,12,198,198]{2,3,1,0:T(8,128)} %get-tuple-element.175, f32[6,12,198]{2,1,0:T(8,128)S(1)} %get-tuple-element.181, f32[6,12,198]{2,1,0:T(8,128)S(1)} %copy-done.16), kind=kLoop, calls=%fused_computation.1 | loop fusion | flops 14113440 | bytes 28340928 | tf_op jit(solution)/shard_map/convert_element_type | solution.py:82
  209.1 9.6 %multiply_reduce_fusion.3 = (bf16[768]{0:T(1024)(128)(2,1)}, f32[6,198]{1,0:T(8,128)S(1)}, f32[6,198]{1,0:T(8,128)S(1)}, bf16[768]{0:T(1024)(128)(2,1)}, f32[6,198,768]{2,1,0:T(8,128)S(1)}) fusion(f32[6,198]{1,0:T(8,128)S(1)} %copy-done.38, f32[6,198]{1,0:T(8,128)S(1)} %copy-done.31, f32[6,1,1,768]{3,2,0,1:T(1,128)} %copy-done.22, ...), kind=kOutput, calls=%fused_computation.38 | convolution fusion | flops 4229808128 | bytes 16337472 | tf_op jit(solution)/shard_map/dot_general | solution.py:22
  246.7 26.7 %reduce-scatter.11.cloned.1.call-done = bf16[6,1,1536]{2,0,1:T(8,128)(2,1)} async-done(((bf16[6,8,1536]{2,0,1:T(8,128)(2,1)}), bf16[6,1,1536]{2,0,1:T(8,128)(2,1)}) %reduce-scatter.11.cloned.1.call-update) | async-done | bytes 18448 | tf_op jit(solution)/shard_map/reduce_scatter | solution.py:206
  292.0 11.0 %bitcast_convert_fusion.2 = bf16[768,2304]{1,0:T(8,128)(2,1)} fusion(bf16[6,198,768]{2,1,0:T(8,128)(2,1)} %copy.209, bf16[6,198,768]{2,1,0:T(8,128)(2,1)} %copy.208, bf16[6,198,768]{2,1,0:T(8,128)(2,1)} %copy.207, f32[768]{0:T(1024)} %param.29, f32[768]{0:T(1024)} %param.28, f32[6,198]{1,0:T(8,128)} %copy-done.37, f32[6,198]{1,0:T(8,128)} %copy-done.30, ...), kind=kOutput, calls=%fused_computation.18 | convolution fusion | flops 4227932160 | bytes 12678432 | tf_op jit(solution)/shard_map/dot_general | solution.py:33
  306.9 11.1 %bitcast_convert_fusion = bf16[3072,768]{1,0:T(8,128)(2,1)} fusion(bf16[6,198,3072]{2,1,0:T(8,128)(2,1)} %get-tuple-element.178, bf16[6,1,198,768]{3,2,1,0:T(8,128)(2,1)} %param.21, f32[6]{0:T(128)} %convert_element_type.298), kind=kOutput, calls=%fused_computation.12 | convolution fusion | flops 5610783744 | bytes 13842456 | tf_op jit(solution)/shard_map/dot_general | solution.py:33
  318.7 12.2 %bitcast_convert_fusion.1 = bf16[768,3072]{1,0:T(8,128)(2,1)} fusion(bf16[6,198,3072]{2,1,0:T(8,128)(2,1)} %get-tuple-element.188, f32[6,198,768]{2,1,0:T(8,128)} %copy-done.7, f32[768]{0:T(1024)} %param.33, f32[768]{0:T(1024)} %param.32, f32[6,198]{1,0:T(8,128)S(1)} %copy-done.40, f32[6,198]{1,0:T(8,128)S(1)} %copy-done.33), kind=kOutput, calls=%fused_computation.13 | convolution fusion | flops 5612608512 | bytes 15682848 | tf_op jit(solution)/shard_map/dot_general | solution.py:33
  332.9 9.4 %reduce-scatter.19.cloned.1.call-done = bf16[192,768]{1,0:T(8,128)(2,1)} async-done(((bf16[768,768]{1,0:T(8,128)(2,1)}), bf16[192,768]{1,0:T(8,128)(2,1)}) %reduce-scatter.19.cloned.1.call-update) | async-done | bytes 294928 | tf_op jit(solution)/shard_map/reduce_scatter | solution.py:252
  342.3 32.2 %reduce-scatter.15.cloned.1.call-done = bf16[192,768]{1,0:T(8,128)(2,1)} async-done(((bf16[768,768]{1,0:T(8,128)(2,1)}), bf16[192,768]{1,0:T(8,128)(2,1)}) %reduce-scatter.15.cloned.1.call-update) | async-done | bytes 294928 | tf_op jit(solution)/shard_map/reduce_scatter | solution.py:240
  374.4 50.5 %reduce-scatter.17.cloned.1.call-done = bf16[192,2304]{1,0:T(8,128)(2,1)} async-done(((bf16[768,2304]{1,0:T(8,128)(2,1)}), bf16[192,2304]{1,0:T(8,128)(2,1)}) %reduce-scatter.17.cloned.1.call-update) | async-done | bytes 884752 | tf_op jit(solution)/shard_map/reduce_scatter | solution.py:249
  424.9 50.5 %reduce-scatter.13.cloned.1.call-done = bf16[192,2304]{1,0:T(8,128)(2,1)} async-done(((bf16[768,2304]{1,0:T(8,128)(2,1)}), bf16[192,2304]{1,0:T(8,128)(2,1)}) %reduce-scatter.13.cloned.1.call-update) | async-done | bytes 884752 | tf_op jit(solution)/shard_map/reduce_scatter | solution.py:237
  475.4 60.4 %reduce-scatter.23.cloned.1.call-done = bf16[768,768]{1,0:T(8,128)(2,1)} async-done(((bf16[3072,768]{1,0:T(8,128)(2,1)}), bf16[768,768]{1,0:T(8,128)(2,1)}) %reduce-scatter.23.cloned.1.call-update) | async-done | bytes 1179664 | tf_op jit(solution)/shard_map/reduce_scatter | solution.py:267
  535.8 60.4 %reduce-scatter.21.cloned.1.call-done = bf16[192,3072]{1,0:T(8,128)(2,1)} async-done(((bf16[768,3072]{1,0:T(8,128)(2,1)}), bf16[192,3072]{1,0:T(8,128)(2,1)}) %reduce-scatter.21.cloned.1.call-update) | async-done | bytes 1179664 | tf_op jit(solution)/shard_map/reduce_scatter | solution.py:261
  604.4 11.5 %fusion.32 = bf16[6,1,198,768]{3,2,1,0:T(8,128)(2,1)} fusion(f32[6,198,768]{2,1,0:T(8,128)} %copy-done.7, f32[768]{0:T(1024)} %param.37, bf16[6,198,3072]{2,1,0:T(8,128)(2,1)} %get-tuple-element.178, bf16[3072,768]{1,0:T(8,128)(2,1)} %param.36), kind=kOutput, calls=%fused_computation.65 | convolution fusion | flops 5608424448 | bytes 17495040 | tf_op jit(solution)/shard_map/dot_general | solution.py:18
  615.9 16.5 %all-reduce.11 = (bf16[768]{0:T(1024)(128)(2,1)}, bf16[768]{0:T(1024)(128)(2,1)}, bf16[768]{0:T(1024)(128)(2,1)}, bf16[768]{0:T(1024)(128)(2,1)}, bf16[768]{0:T(...) all-reduce(bf16[768]{0:T(1024)(128)(2,1)} %get-tuple-element.163, ...), channel_id=5, replica_groups=mesh['frame'=8,'video'=4] {'video'}, use_global_device_ids=true, to_apply=%region_24.0.clone | all-reduce | flops 9216 | bytes 36864
  643.3 15.5 %all-reduce.9 = (bf16[192]{0:T(256)(128)(2,1)}, bf16[192]{0:T(256)(128)(2,1)}, bf16[192]{0:T(256)(128)(2,1)}, bf16[192]{0:T(256)(128)(2,1)}, bf16[192]{0:T(256)(...) all-reduce(bf16[192]{0:T(256)(128)(2,1)} %dynamic-slice.1, ...), channel_id=1, replica_groups=mesh['frame'=8,'video'=4] {'frame'}, use_global_device_ids=true, to_apply=%region_25.0 | all-reduce | flops 2304 | bytes 9216 | tf_op jit(solution)/shard_map/psum | solution.py:277
  675.7 40.9 %all-reduce.14.cloned.1.call-done = (bf16[192,768]{0,1:T(8,128)(2,1)}, bf16[192,2304]{1,0:T(8,128)(2,1)}, bf16[192,768]{1,0:T(8,128)(2,1)}, bf16[192,2304]{1,0:T...) async-done(((bf16[192,768]{0,1:T(8,128)(2,1)}, bf16[192,2304]{1,0:T(8,128)(2,1)}, bf16[192,768]{1,0:T(8,128)(2,1)}, ...) | async-done | bytes 5013520 | tf_op jit(solution)/shard_map/psum | solution.py:276
  (257 shorter events, 198.0 us)
Async XLA Ops:
  7.2 50.0 %copy-start = (bf16[768,2304]{1,0:T(8,128)(2,1)S(1)}, bf16[768,2304]{1,0:T(8,128)(2,1)}, u32[]{:S(2)}) copy-start(bf16[768,2304]{1,0:T(8,128)(2,1)} %param.30) | copy-start | bytes 10616836
  7.2 266.2 %reduce-scatter.11.cloned.1.call-start = ((), (), s32[]{:S(2)}) async-start(), calls=%async_computation.8 | async-start | bytes 221184 | tf_op jit(solution)/shard_map/reduce_scatter | solution.py:206
  10.6 41.8 %copy-start.20 = (bf16[6,768]{1,0:T(8,128)(2,1)}, bf16[6,768]{1,0:T(8,128)(2,1)S(1)}, u32[]{:S(2)}) copy-start(bf16[6,768]{1,0:T(8,128)(2,1)S(1)} %get-tuple-element.173) | copy-start | bytes 27652
  11.6 25.2 %copy-start.34 = (f32[768]{0:T(1024)S(1)}, f32[768]{0:T(1024)}, u32[]{:S(2)}) copy-start(f32[768]{0:T(1024)} %param.24) | copy-start | bytes 9220
  16.7 19.3 %copy-start.55 = (s32[6]{0:T(128)S(1)}, s32[6]{0:T(128)}, u32[]{:S(2)}) copy-start(s32[6]{0:T(128)} %param.20) | copy-start | bytes 76
  16.7 20.1 %copy-start.14 = (bf16[768,2304]{1,0:T(8,128)(2,1)S(1)}, bf16[768,2304]{1,0:T(8,128)(2,1)}, u32[]{:S(2)}) copy-start(bf16[768,2304]{1,0:T(8,128)(2,1)} %param.26) | copy-start | bytes 10616836
  16.7 20.1 %copy-start.41 = (f32[768]{0:T(1024)S(1)}, f32[768]{0:T(1024)}, u32[]{:S(2)}) copy-start(f32[768]{0:T(1024)} %param.25) | copy-start | bytes 9220
  110.4 37.8 %copy-start.7 = (f32[6,198,768]{2,1,0:T(8,128)}, f32[6,198,768]{2,1,0:T(8,128)S(1)}, u32[]{:S(2)}) copy-start(f32[6,198,768]{2,1,0:T(8,128)S(1)} %get-tuple-element.177) | copy-start | bytes 10948612
  110.5 37.7 %copy-start.32 = (f32[6,198]{1,0:T(8,128)}, f32[6,198]{1,0:T(8,128)S(1)}, u32[]{:S(2)}) copy-start(f32[6,198]{1,0:T(8,128)S(1)} %broadcast_multiply_fusion.4) | copy-start | bytes 14260
  111.3 36.9 %copy-start.39 = (f32[6,198]{1,0:T(8,128)}, f32[6,198]{1,0:T(8,128)S(1)}, u32[]{:S(2)}) copy-start(f32[6,198]{1,0:T(8,128)S(1)} %add_rsqrt_fusion) | copy-start | bytes 14260
  111.3 11.9 %copy-start.13 = (bf16[6,1,198,768]{3,2,1,0:T(8,128)(2,1)S(1)}, bf16[6,1,198,768]{3,2,1,0:T(8,128)(2,1)}, u32[]{:S(2)}) copy-start(bf16[6,1,198,768]{3,2,1,0:T(8,128)(2,1)} %param.21) | copy-start | bytes 5474308
  111.3 11.9 %copy-start.48 = (f32[6]{0:T(128)S(1)}, f32[6]{0:T(128)}, u32[]{:S(2)}) copy-start(f32[6]{0:T(128)} %convert_element_type.298) | copy-start | bytes 76
  222.3 51.1 %copy-start.21 = (bf16[6,768]{1,0:T(8,128)(2,1)S(1)}, bf16[6,768]{1,0:T(8,128)(2,1)}, u32[]{:S(2)}) copy-start(bf16[6,768]{1,0:T(8,128)(2,1)} %copy-done.20) | copy-start | bytes 27652
  222.3 51.1 %copy-start.35 = (f32[768]{0:T(1024)S(1)}, f32[768]{0:T(1024)}, u32[]{:S(2)}) copy-start(f32[768]{0:T(1024)} %param.24) | copy-start | bytes 9220
  242.0 89.1 %reduce-scatter.25.cloned.1.call-start = ((), (), s32[]{:S(2)}) async-start(), calls=%async_computation.15 | async-start | bytes 1474560
  283.1 59.2 %reduce-scatter.19.cloned.1.call-start = ((), (), s32[]{:S(2)}) async-start(), calls=%async_computation.12 | async-start | bytes 1474560 | tf_op jit(solution)/shard_map/reduce_scatter | solution.py:252
  288.7 85.7 %reduce-scatter.15.cloned.1.call-start = ((), (), s32[]{:S(2)}) async-start(), calls=%async_computation.10 | async-start | bytes 1474560 | tf_op jit(solution)/shard_map/reduce_scatter | solution.py:240
  292.0 133.0 %reduce-scatter.17.cloned.1.call-start = ((), (), s32[]{:S(2)}) async-start(), calls=%async_computation.11 | async-start | bytes 4423680 | tf_op jit(solution)/shard_map/reduce_scatter | solution.py:249
  303.0 172.4 %reduce-scatter.13.cloned.1.call-start = ((), (), s32[]{:S(2)}) async-start(), calls=%async_computation.9 | async-start | bytes 4423680 | tf_op jit(solution)/shard_map/reduce_scatter | solution.py:237
  306.9 228.9 %reduce-scatter.23.cloned.1.call-start = ((), (), s32[]{:S(2)}) async-start(), calls=%async_computation.14 | async-start | bytes 5898240 | tf_op jit(solution)/shard_map/reduce_scatter | solution.py:267
  318.0 278.1 %reduce-scatter.21.cloned.1.call-start = ((), (), s32[]{:S(2)}) async-start(), calls=%async_computation.13 | async-start | bytes 5898240 | tf_op jit(solution)/shard_map/reduce_scatter | solution.py:261
  331.0 385.7 %all-reduce.14.cloned.1.call-start = ((), (), s32[]{:S(2)}) async-start(), calls=%async_computation.16 | async-start | bytes 10223616 | tf_op jit(solution)/shard_map/psum | solution.py:276
  604.4 11.5 %copy-start.44 = (bf16[768]{0:T(1024)(128)(2,1)S(1)}, bf16[768]{0:T(1024)(128)(2,1)}, u32[]{:S(2)}) copy-start(bf16[768]{0:T(1024)(128)(2,1)} %get-tuple-element.134) | copy-start | bytes 4612
  604.4 65.4 %copy-start.27 = (bf16[6,768]{1,0:T(8,128)(2,1)S(1)}, bf16[6,768]{1,0:T(8,128)(2,1)}, u32[]{:S(2)}) copy-start(bf16[6,768]{1,0:T(8,128)(2,1)} %copy-done.26) | copy-start | bytes 27652
  (44 other events, 224.5 us)
Sparse Core Ops, SparseCore 0:
  242.1 31.2 reduce-scatter.10
  283.2 26.6 reduce-scatter.24
  313.7 28.5 reduce-scatter.18
  345.9 28.5 reduce-scatter.14
  377.7 47.2 reduce-scatter.16
  428.2 47.2 reduce-scatter.12
  478.7 57.0 reduce-scatter.22
  539.0 57.0 reduce-scatter.20
  600.0 116.6 all-reduce.13
where the time goes:
time: 745 us; the launch traced here: 736 us
  waiting for transfers between devices  331 us (44%)
  matrix products  183 us (25%)
  local copies, waits for them, and re-layouts  85.2 us (11%)
  other arithmetic  73 us (10%)
  blocking collectives  47.7 us (6%)
  between operations  16.2 us (2%)
    reduce_scatter x1, waiting for transfers between devices, local(): lax.psum_scatter(grad_dense_out.astype(jnp.bfloat16), 'video', scatter_di...  60.4 us
    reduce_scatter x1, waiting for transfers between devices, local(): lax.psum_scatter(grad_dense_in.astype(jnp.bfloat16), 'video', scatter_dim...  60.4 us
    reduce_scatter x1, waiting for transfers between devices, local(): lax.psum_scatter(grad_message_qkv.astype(jnp.bfloat16), 'video', scatter_...  50.5 us
    reduce_scatter x1, waiting for transfers between devices, local(): lax.psum_scatter(grad_frame_qkv.astype(jnp.bfloat16), 'video', scatter_di...  50.5 us
    dot_general x7, matrix products, weight_grad(): lax.dot_general(left, right, (((0,), (0,)), ((), ())), preferred_element_...  47.4 us
    dot_general x7, matrix products, back_matmul(): lax.dot_general(grad_low, weight, (((grad_low.ndim - 1,), (1,)), ((), ())...  44 us
    psum x1, waiting for transfers between devices, local(): lax.psum(shares[0].astype(jnp.bfloat16), 'frame').astype(jnp.float32)  40.9 us
    dot_general x8, matrix products, matmul(): return jnp.dot(left, right, preferred_element_type=jnp.float32)  38.5 us
  transfers between devices with their start and end apart: 9, of which 8 were waited for; matrix products, arithmetic and copies ran while one was open for 14% of the time, Pallas kernels for 0%

commit v1 on v0

v1 whole, which is shorter than its diff:
```python
import functools
import jax
import jax.numpy as jnp
from jax import lax
from jax.experimental import pallas as pl
from jax.experimental.pallas import tpu as pltpu
bf=jnp.bfloat16; f32=jnp.float32
EPS=1e-5
def dot(a,b,ca=1,cb=0): return lax.dot_general(a,b,(((ca,),(cb,)),((),())),preferred_element_type=f32)
FR=6; T=208; RR=FR*T; RP=1280; D=768
def k2(MB, mid, cot, live, din0,din1,din2,din3, do0,do1,do2,do3, bin_, bout, gain, shift,
       out_ref, gmid_ref, gdi_ref, gdo_ref, gbin_ref, small_ref,
       sec, G, act, dinn, oacc, gsec):
    j=pl.program_id(0)
    @pl.when(j==0)
    def _():
        ob=jnp.zeros((1,D),f32)
        sec[pl.ds(RR,RP-RR),:]=jnp.zeros((RP-RR,D),bf)
        G[pl.ds(RR,RP-RR),:]=jnp.zeros((RP-RR,D),bf)
        act[pl.ds(RR,RP-RR),:]=jnp.zeros((RP-RR,512),bf)
        dinn[pl.ds(RR,RP-RR),:]=jnp.zeros((RP-RR,512),bf)
        for f in range(FR):
            x=mid[f*T:(f+1)*T,:]
            mu=jnp.mean(x,-1,keepdims=True); c=x-mu
            inv=lax.rsqrt(jnp.mean(c*c,-1,keepdims=True)+EPS)
            sec[f*T:(f+1)*T,:]=(c*inv*gain[...]+shift[...]).astype(bf)
            g=cot[f,0].astype(f32)*live[f].astype(f32)
            g=jnp.concatenate([g,jnp.zeros((T-198,D),f32)],0)
            ob=ob+jnp.sum(g,0,keepdims=True)
            G[f*T:(f+1)*T,:]=g.astype(bf)
            oacc[f*T:(f+1)*T,:]=x+bout[...]
            gsec[f*T:(f+1)*T,:]=jnp.zeros((T,D),f32)
        small_ref[0:1,:]=ob
    din=jnp.concatenate([din0[...],din1[...],din2[...],din3[...]],1)
    do=jnp.concatenate([do0[...],do1[...],do2[...],do3[...]],0)
    b=jnp.concatenate([bin_[0:1,:],bin_[1:2,:],bin_[2:3,:],bin_[3:4,:]],1) if False else bin_[0]
    bsum=jnp.zeros((1,512),f32)
    for r in range(RR//MB):
        s=slice(r*MB,(r+1)*MB)
        inner=dot(sec[s,:],din)+b
        ga=dot(G[s,:],do,1,1)
        sg=0.5*jnp.tanh(0.851*inner)+0.5
        ac=inner*sg
        act[s,:]=ac.astype(bf)
        di=ga*(sg+1.702*ac*(1.0-sg))
        bsum=bsum+jnp.sum(di,0,keepdims=True)
        dinn[s,:]=di.astype(bf)
    gbin_ref[0]=bsum
    for r in range(RR//MB):
        s=slice(r*MB,(r+1)*MB)
        oacc[s,:]+=dot(act[s,:],do)
        gsec[s,:]+=dot(dinn[s,:],din,1,1)
    gdo_ref[0]=dot(G[...],act[...],0,0).astype(bf)
    gdi_ref[0]=dot(sec[...],dinn[...],0,0).astype(bf)
    @pl.when(j==pl.num_programs(0)-1)
    def _():
        gg=jnp.zeros((1,D),f32); gs=jnp.zeros((1,D),f32)
        for f in range(FR):
            s=slice(f*T,(f+1)*T)
            out_ref[f,0]=oacc[s,:][:198].astype(bf)
            x=mid[s,:]
            mu=jnp.mean(x,-1,keepdims=True); c=x-mu
            inv=lax.rsqrt(jnp.mean(c*c,-1,keepdims=True)+EPS)
            sc=c*inv
            go=gsec[s,:]
            gg=gg+jnp.sum(go*sc,0,keepdims=True); gs=gs+jnp.sum(go,0,keepdims=True)
            gsc=go*gain[...]
            gi=inv*(gsc-jnp.mean(gsc,-1,keepdims=True)-sc*jnp.mean(gsc*sc,-1,keepdims=True))
            gmid_ref[s,:]=G[s,:].astype(f32)+gi
        small_ref[1:2,:]=gg; small_ref[2:3,:]=gs
def call_k2(mid,cot,live,din,do,bin_,bout,gain,shift,MB=624):
    full=lambda *s: pl.BlockSpec(s,lambda j:(0,)*len(s))
    nq=din.shape[1]//512
    vm=pl.BlockSpec(memory_space=pltpu.VMEM)
    specs=[full(RR,D),full(FR,1,198,D),pl.BlockSpec(memory_space=pltpu.SMEM)]
    for q in range(4): specs.append(pl.BlockSpec((D,128),lambda j,q=q:(0,q*6+j)))
    for q in range(4): specs.append(pl.BlockSpec((128,D),lambda j,q=q:(q*6+j,0)))
    specs+= [pl.BlockSpec((1,1,512),lambda j:(j,0,0)),full(1,D),full(1,D),full(1,D)]
    b3=bin_.reshape(4,6,128).transpose(1,0,2).reshape(6,1,512)
    return pl.pallas_call(functools.partial(k2,MB),grid=(6,),in_specs=specs,
      out_specs=[full(FR,1,198,D),full(RR,D),pl.BlockSpec((1,D,512),lambda j:(j,0,0)),pl.BlockSpec((1,D,512),lambda j:(j,0,0)),pl.BlockSpec((1,1,512),lambda j:(j,0,0)),full(8,D)],
      out_shape=[jax.ShapeDtypeStruct((FR,1,198,D),bf),jax.ShapeDtypeStruct((RR,D),f32),jax.ShapeDtypeStruct((6,D,512),bf),jax.ShapeDtypeStruct((6,D,512),bf),jax.ShapeDtypeStruct((6,1,512),f32),jax.ShapeDtypeStruct((8,D),f32)],
      scratch_shapes=[pltpu.VMEM((RP,D),bf),pltpu.VMEM((RP,D),bf),pltpu.VMEM((RP,512),bf),pltpu.VMEM((RP,512),bf),pltpu.VMEM((RR,D),f32),pltpu.VMEM((RR,D),f32)],
      compiler_params=pltpu.CompilerParams(vmem_limit_bytes=61<<20,dimension_semantics=("arbitrary",)),
    )(mid,cot,live,din,din,din,din,do,do,do,do,b3,bout.reshape(1,D),gain.reshape(1,D),shift.reshape(1,D))
from jax.sharding import PartitionSpec as P
HEADS=12
HEAD_DIM=64
NEG=-1e30

def half_masks(rows):
    lane=lax.broadcasted_iota(jnp.int32,(rows,128),1)
    return lane<64
def k1(vid, mnext, wq, wk, wv, wo, gain, shift,
       qkv_ref, pt_ref, first_ref, mixed_ref, mid_ref):
    h=pl.program_id(0)
    @pl.when(h==0)
    def _():
        first_ref[pl.ds(RR,RP-RR),:]=jnp.zeros((RP-RR,D),bf)
        mixed_ref[:,pl.ds(RR,RP-RR),:]=jnp.zeros((6,RP-RR,128),bf)
        for f in range(FR):
            mid_ref[f*T+192:(f+1)*T,:]=jnp.zeros((T-192,D),f32)
            mid_ref[f*T:f*T+197,:]=vid[f,0].astype(f32)
            mid_ref[f*T+197:f*T+198,:]=mnext[f:f+1,:]
            x=mid_ref[f*T:(f+1)*T,:]
            mu=jnp.mean(x,-1,keepdims=True); c=x-mu
            inv=lax.rsqrt(jnp.mean(c*c,-1,keepdims=True)+EPS)
            first_ref[f*T:(f+1)*T,:]=(c*inv*gain[...]+shift[...]).astype(bf)
    w=jnp.concatenate([wq[...],wk[...],wv[...]],1)
    qkv_ref[0,0:RR,:]=dot(first_ref[0:RR,:],w).astype(bf)
    qkv_ref[0,RR:RP,:]=jnp.zeros((RP-RR,384),bf)
    lo=half_masks(T)
    keep=lax.broadcasted_iota(jnp.int32,(16,T),0)<6
    zero=jnp.zeros((T,128),bf)
    for f in range(FR):
        s=slice(f*T,(f+1)*T)
        q=qkv_ref[0,s,0:128]*jnp.asarray(0.125,bf); k=qkv_ref[0,s,128:256]; v=qkv_ref[0,s,256:384]
        ps=[]; vs=[]
        for e in range(2):
            m=lo if e==0 else jnp.logical_not(lo)
            st=dot(k,jnp.where(m,q,zero),1,1)
            top=st[:192]; bot=jnp.where(keep,st[192:],NEG)
            mx=jnp.maximum(jnp.max(top,0,keepdims=True),jnp.max(bot,0,keepdims=True))
            top=jnp.exp(top-mx); bot=jnp.exp(bot-mx)
            tot=jnp.sum(top,0,keepdims=True)+jnp.sum(bot,0,keepdims=True)
            p=(jnp.concatenate([top,bot],0)*(1.0/tot)).astype(bf)
            pt_ref[0,f*2+e]=p
            ps.append(p); vs.append(jnp.where(m,v,zero))
        o=dot(jnp.concatenate(ps,0),jnp.concatenate(vs,0),0,0)
        mixed_ref[h,s,:]=o.astype(bf)
    @pl.when(h==5)
    def _():
        mx=jnp.concatenate([mixed_ref[i,0:RR,:] for i in range(6)],1)
        mid_ref[...]+=dot(mx,wo[...])
def call_k1(video,mnext,qkv,wo,gain,shift):
    full=lambda *s: pl.BlockSpec(s,lambda j:(0,)*len(s))
    blk=lambda *s: pl.BlockSpec((1,)+s,lambda j:(j,)+(0,)*len(s))
    specs=[full(FR,1,197,D),full(FR,D)]+[pl.BlockSpec((D,128),lambda j,o=o:(0,o*6+j)) for o in range(3)]+[full(D,D),full(1,D),full(1,D)]
    return pl.pallas_call(k1,grid=(6,),in_specs=specs,
      out_specs=[blk(RP,384),blk(12,T,T),full(RP,D),full(6,RP,128),full(RR,D)],
      out_shape=[jax.ShapeDtypeStruct((6,RP,384),bf),jax.ShapeDtypeStruct((6,12,T,T),bf),jax.ShapeDtypeStruct((RP,D),bf),jax.ShapeDtypeStruct((6,RP,128),bf),jax.ShapeDtypeStruct((RR,D),f32)],
      compiler_params=pltpu.CompilerParams(vmem_limit_bytes=61<<20,dimension_semantics=("arbitrary",)),
    )(video,mnext,qkv,qkv,qkv,wo,gain.reshape(1,D),shift.reshape(1,D))
def k3(vid, mnext, gmid, qkv, pt, first, mixed, wq, wk, wv, wo, gain, shift,
       gtok_ref, gf_ref, small_ref, glow, dO, dpk, wqkv):
    h=pl.program_id(0)
    @pl.when(h==0)
    def _():
        glow[pl.ds(RR,RP-RR),:]=jnp.zeros((RP-RR,D),bf)
        dpk[:,pl.ds(RR,RP-RR),:]=jnp.zeros((6,RP-RR,384),bf)
        glow[0:RR,:]=gmid[...].astype(bf)
        d=dot(glow[0:RR,:],wo[...],1,1).astype(bf)
        for i in range(6): dO[i]=d[:,i*128:(i+1)*128]
    lo=half_masks(T)
    zero=jnp.zeros((T,128),bf)
    for f in range(FR):
        s=slice(f*T,(f+1)*T)
        q=qkv[0,s,0:128]; k=qkv[0,s,128:256]; v=qkv[0,s,256:384]
        do=dO[h,s,:]
        dss=[]; ks=[]; dk=0.; dv=0.
        for e in range(2):
            m=lo if e==0 else jnp.logical_not(lo)
            doe=jnp.where(m,do,zero)
            pb=pt[0,f*2+e]
            p=pb.astype(f32)
            dp=dot(v,doe,1,1)
            delta=jnp.sum(dp*p,0,keepdims=True)
            ds=(p*(dp-delta)).astype(bf)
            dk=dk+dot(ds,jnp.where(m,q,zero))
            dv=dv+dot(pb,doe)
            dss.append(ds); ks.append(jnp.where(m,k,zero))
        dq=dot(jnp.concatenate(dss,0),jnp.concatenate(ks,0),0,0)*0.125
        dpk[h,s,0:128]=dq.astype(bf)
        dpk[h,s,128:256]=(dk*0.125).astype(bf)
        dpk[h,s,256:384]=dv.astype(bf)
    for i in range(6):
        @pl.when(h==i)
        def _():
            wqkv[:,i*128:(i+1)*128]=wq[...]; wqkv[:,D+i*128:D+(i+1)*128]=wk[...]; wqkv[:,2*D+i*128:2*D+(i+1)*128]=wv[...]
            mx=jnp.concatenate([mixed[t] for t in range(6)],1)
            gf_ref[0,:,384:512]=dot(mx,glow[:,i*128:(i+1)*128],0,0).astype(bf)
    gf_ref[0,:,0:384]=dot(first[...],dpk[h],0,0).astype(bf)
    @pl.when(h==5)
    def _():
        dx=jnp.concatenate([dpk[i,0:RR,g*128:(g+1)*128] for g in range(3) for i in range(6)],1)
        gtok_ref[...]=dot(dx,wqkv[...],1,1)
        gg=jnp.zeros((1,D),f32); gs=jnp.zeros((1,D),f32)
        for f in range(FR):
            s=slice(f*T,(f+1)*T)
            x=jnp.concatenate([vid[f,0].astype(f32),mnext[f:f+1,:],jnp.zeros((T-198,D),f32)],0)
            mu=jnp.mean(x,-1,keepdims=True); c=x-mu
            inv=lax.rsqrt(jnp.mean(c*c,-1,keepdims=True)+EPS)
            sc=c*inv
            go=gtok_ref[s,:]
            gg=gg+jnp.sum(go*sc,0,keepdims=True); gs=gs+jnp.sum(go,0,keepdims=True)
            gsc=go*gain[...]
            gi=inv*(gsc-jnp.mean(gsc,-1,keepdims=True)-sc*jnp.mean(gsc*sc,-1,keepdims=True))
            gtok_ref[s,:]=gmid[s,:]+gi
        small_ref[0:1,:]=gg; small_ref[1:2,:]=gs
def call_k3(video,mnext,gmid,qkvs,pt,first,mixed,qkv,wo,gain):
    full=lambda *s: pl.BlockSpec(s,lambda j:(0,)*len(s))
    blk=lambda *s: pl.BlockSpec((1,)+s,lambda j:(j,)+(0,)*len(s))
    specs=[full(FR,1,197,D),full(FR,D),full(RR,D),blk(RP,384),blk(12,T,T),full(RP,D),full(6,RP,128)]+[pl.BlockSpec((D,128),lambda j,o=o:(0,o*6+j)) for o in range(3)]+[full(D,D),full(1,D),full(1,D)]
    return pl.pallas_call(k3,grid=(6,),in_specs=specs,
      out_specs=[full(RR,D),blk(D,512),full(8,D)],
      out_shape=[jax.ShapeDtypeStruct((RR,D),f32),jax.ShapeDtypeStruct((6,D,512),bf),jax.ShapeDtypeStruct((8,D),f32)],
      scratch_shapes=[pltpu.VMEM((RP,D),bf),pltpu.VMEM((6,RR,128),bf),pltpu.VMEM((6,RP,384),bf),pltpu.VMEM((D,3*D),bf)],
      compiler_params=pltpu.CompilerParams(vmem_limit_bytes=61<<20,dimension_semantics=("arbitrary",)),
    )(video,mnext,gmid,qkvs,pt,first,mixed,qkv,qkv,qkv,wo,gain.reshape(1,D),gain.reshape(1,D))


def column_sum(values):
    return jnp.sum(values.reshape(-1, values.shape[-1]), axis=0)


def matmul(left, right):
    return jnp.dot(left, right, preferred_element_type=f32)


def back_matmul(grad_low, weight):
    return lax.dot_general(grad_low, weight, (((grad_low.ndim - 1,), (1,)), ((), ())), preferred_element_type=f32)


def weight_grad(inputs_low, grad_low):
    left = inputs_low.reshape(-1, inputs_low.shape[-1])
    right = grad_low.reshape(-1, grad_low.shape[-1])
    return lax.dot_general(left, right, (((0,), (0,)), ((), ())), preferred_element_type=f32)


def norm_forward(values, gain, shift):
    center = values - jnp.mean(values, axis=-1, keepdims=True)
    inverse = lax.rsqrt(jnp.mean(center * center, axis=-1, keepdims=True) + EPS)
    scaled = center * inverse
    return (scaled * gain + shift, scaled, inverse)


def norm_backward(grad_out, scaled, inverse, gain):
    grad_scaled = grad_out * gain
    grad_in = inverse * (
        grad_scaled
        - jnp.mean(grad_scaled, axis=-1, keepdims=True)
        - scaled * jnp.mean(grad_scaled * scaled, axis=-1, keepdims=True)
    )
    return (grad_in, column_sum(grad_out * scaled), column_sum(grad_out))


def split_heads(values):
    return values.reshape(values.shape[:-1] + (HEADS, HEAD_DIM))


def attend_forward(query_rows, key_rows, value_rows):
    scores = jnp.einsum("bqhd,bkhd->bhqk", query_rows, key_rows, preferred_element_type=f32) * 0.125
    largest = jnp.max(scores, axis=-1, keepdims=True)
    raised = jnp.exp(scores - largest)
    total = jnp.sum(raised, axis=-1, keepdims=True)
    probs_low = (raised / total).astype(bf)
    mixed = jnp.einsum("bhqk,bkhd->bqhd", probs_low, value_rows, preferred_element_type=f32)
    return (mixed, largest + jnp.log(total))


def attend_backward(query_rows, key_rows, value_rows, log_total, grad_mixed):
    scores = jnp.einsum("bqhd,bkhd->bhqk", query_rows, key_rows, preferred_element_type=f32) * 0.125
    probs = jnp.exp(scores - log_total)
    grad_probs = jnp.einsum("bqhd,bkhd->bhqk", grad_mixed, value_rows, preferred_element_type=f32)
    grad_scores = probs * (grad_probs - jnp.sum(grad_probs * probs, axis=-1, keepdims=True))
    grad_low = grad_scores.astype(bf)
    grad_query = jnp.einsum("bhqk,bkhd->bqhd", grad_low, key_rows, preferred_element_type=f32) * 0.125
    grad_key = jnp.einsum("bhqk,bqhd->bkhd", grad_low, query_rows, preferred_element_type=f32) * 0.125
    grad_value = jnp.einsum("bhqk,bqhd->bkhd", probs.astype(bf), grad_mixed, preferred_element_type=f32)
    return (grad_query, grad_key, grad_value)


def message_forward(video, message_proj, message_bias, message_gain, message_shift, message_qkv, message_out):
    width = video.shape[-1]
    batch, frames_local = video.shape[:2]
    class_rows = video[:, :, 0, :]
    message = (matmul(class_rows, message_proj) + message_bias).astype(bf)
    message_wide = message.astype(f32)
    normed_own, scaled_own, inverse_own = norm_forward(message_wide, message_gain, message_shift)
    normed_low = normed_own.astype(bf)
    everyone = lax.all_gather(message, "frame", axis=1, tiled=True)
    normed_all = norm_forward(everyone.astype(f32), message_gain, message_shift)[0]
    key_value = matmul(normed_all.astype(bf), message_qkv[:, width:]).astype(bf)
    query = split_heads(matmul(normed_low, message_qkv[:, :width]).astype(bf))
    key = split_heads(key_value[..., :width])
    value = split_heads(key_value[..., width:])
    mixed, total = attend_forward(query, key, value)
    mixed_low = mixed.reshape(batch, frames_local, width).astype(bf)
    message_next = message_wide + matmul(mixed_low, message_out)
    return message_next, (class_rows, normed_low, scaled_own, inverse_own, query, key, value, mixed_low, total)


def message_backward(kept, grad_next, message_proj, message_gain, message_qkv, message_out):
    class_rows, normed_low, scaled_own, inverse_own, query, key, value, mixed_low, total = kept
    batch, frames_local, width = grad_next.shape
    frames_all = key.shape[1]
    grad_next_low = grad_next.astype(bf)
    grad_mixed = split_heads(back_matmul(grad_next_low, message_out).astype(bf))
    grad_q, grad_k, grad_v = attend_backward(query, key, value, total, grad_mixed)
    key_value_grad = jnp.concatenate(
        [grad_k.reshape(batch, frames_all, width), grad_v.reshape(batch, frames_all, width)], axis=-1
    )
    own = lax.psum_scatter(key_value_grad.astype(bf), "frame", scatter_dimension=1, tiled=True)
    packed = jnp.concatenate([grad_q.reshape(batch, frames_local, width).astype(bf), own], axis=-1)
    grad_in, grad_gain, grad_shift = norm_backward(
        back_matmul(packed, message_qkv), scaled_own, inverse_own, message_gain
    )
    grad_message = grad_next + grad_in
    grad_message_low = grad_message.astype(bf)
    grad_class = back_matmul(grad_message_low, message_proj)
    rows = jnp.concatenate([class_rows, normed_low, mixed_low, grad_message_low, packed, grad_next_low], axis=-1)
    rows = rows.reshape(batch * frames_local, -1)
    return grad_class, rows, column_sum(grad_message), grad_gain, grad_shift


def local(
    video,
    video_live,
    cotangent,
    message_proj,
    message_bias,
    message_gain,
    message_shift,
    message_qkv,
    message_out,
    frame_gain,
    frame_shift,
    frame_qkv,
    frame_out,
    dense_gain,
    dense_shift,
    dense_in,
    dense_in_bias,
    dense_out,
    dense_out_bias,
):
    batch, frames_local, patches, width = video.shape
    hidden = dense_in.shape[1]
    groups = lax.axis_size("video")
    message_next, kept = message_forward(
        video, message_proj, message_bias, message_gain, message_shift, message_qkv, message_out
    )
    next_rows = message_next.reshape(batch * frames_local, width)
    packed, probs, first, mixed, middle = call_k1(video, next_rows, frame_qkv, frame_out, frame_gain, frame_shift)
    output, grad_middle, part_in, part_out, part_bias, dense_small = call_k2(
        middle, cotangent, video_live, dense_in, dense_out, dense_in_bias, dense_out_bias, dense_gain, dense_shift
    )
    grad_tokens, part_frame, frame_small = call_k3(
        video, next_rows, grad_middle, packed, probs, first, mixed, frame_qkv, frame_out, frame_gain
    )
    grad_tokens = grad_tokens.reshape(batch, frames_local, T, width)
    grad_next = grad_tokens[:, :, patches]
    grad_class, rows, sum_bias, sum_gain, sum_shift = message_backward(
        kept, grad_next, message_proj, message_gain, message_qkv, message_out
    )
    grad_input = jnp.concatenate(
        [grad_tokens[:, :, :1] + grad_class[:, :, None, :], grad_tokens[:, :, 1:patches]], axis=2
    ).astype(bf)

    def total(value):
        share = lax.psum_scatter(value, "video", scatter_dimension=0, tiled=True)
        return lax.psum(share, "frame").astype(f32)

    grad_in = total(part_in.reshape(6, width, 4, 128).transpose(1, 2, 0, 3).reshape(width, hidden))
    grad_out = total(part_out.reshape(6, width, 4, 128).transpose(2, 0, 3, 1).reshape(hidden, width))
    part_frame = part_frame.reshape(6, width, 4, 128).transpose(1, 2, 0, 3).reshape(width, 4 * width)
    grad_frame = total(part_frame)
    vector = jnp.concatenate(
        [
            sum_bias,
            sum_gain,
            sum_shift,
            frame_small[0],
            frame_small[1],
            dense_small[1],
            dense_small[2],
            dense_small[0],
            part_bias.reshape(6, 4, 128).transpose(1, 0, 2).reshape(hidden),
        ]
    )
    vector = lax.psum(vector, ("video", "frame"))
    place = lax.axis_index("video")
    cut = width // groups

    def mine(start, length):
        return lax.dynamic_slice_in_dim(vector, start + place * (length // groups), length // groups)

    gathered = lax.all_gather(rows, ("video", "frame"), axis=0, tiled=True)

    def outer(left, first_column, last_column):
        part = lax.dynamic_slice_in_dim(gathered, left * width + place * cut, cut, axis=1)
        return weight_grad(part, gathered[:, first_column:last_column])

    return (
        output,
        grad_input,
        outer(0, 3 * width, 4 * width),
        mine(0, width),
        mine(width, width),
        mine(2 * width, width),
        outer(1, 4 * width, 7 * width),
        outer(2, 7 * width, 8 * width),
        mine(3 * width, width),
        mine(4 * width, width),
        grad_frame[:, : 3 * width],
        grad_frame[:, 3 * width :],
        mine(5 * width, width),
        mine(6 * width, width),
        grad_in,
        mine(8 * width, hidden),
        grad_out,
        mine(7 * width, width),
    )


def solution(mesh):
    in_specs = (
        P("video", "frame", None, None),
        P("video"),
        P("video", "frame", None, None),
        P(),
        P(),
        P(),
        P(),
        P(),
        P(),
        P(),
        P(),
        P(),
        P(),
        P(),
        P(),
        P(),
        P(),
        P(),
        P(),
    )
    out_specs = (
        P("video", "frame", None, None),
        P("video", "frame", None, None),
        P("video", None),
        P("video"),
        P("video"),
        P("video"),
        P("video", None),
        P("video", None),
        P("video"),
        P("video"),
        P("video", None),
        P("video", None),
        P("video"),
        P("video"),
        P("video", None),
        P("video"),
        P("video", None),
        P("video"),
    )
    return jax.shard_map(local, mesh=mesh, in_specs=in_specs, out_specs=out_specs, check_vma=False)
```

time: 745 us -> 570 us (0.77)
  matrix products: 183 us -> 14.6 us
  Pallas kernels: 0 us -> 124 us
  waiting for transfers between devices: 331 us -> 251 us
  other arithmetic: 73 us -> 5.94 us
  local copies, waits for them, and re-layouts: 85.2 us -> 95.5 us
  blocking collectives: 47.7 us -> 55.6 us
    reduce_scatter x7 -> x2, waiting for transfers between devices: 290 us -> 57.7 us  [the longest x1 57.7 us: total(): share = lax.psum_scatter(value, 'video', scatter_dimension=0, tiled=True)]
    pallas_call x0 -> x3, Pallas kernels: none -> 124 us  [the longest x1 51.2 us: call_k2(): pl.pallas_call(functools.partial(k2, MB), grid=(6,), in_specs=specs, out_...]
    unnamed x10 -> x8, waiting for transfers between devices: 0.17 us -> 75.6 us
    psum x1, waiting for transfers between devices: 40.9 us -> 92.7 us  [total(): return lax.psum(share, 'frame').astype(f32)]
    dot_general x10 -> x4, matrix products: 52.5 us -> 5.89 us  [matmul(): return jnp.dot(left, right, preferred_element_type=f32)]
    dot_general x7 -> x3, matrix products: 47.4 us -> 3.8 us  [weight_grad(): lax.dot_general(left, right, (((0,), (0,)), ((), ())), preferred_element_...]
    dot_general x7 -> x3, matrix products: 44 us -> 4.09 us  [back_matmul(): lax.dot_general(grad_low, weight, (((grad_low.ndim - 1,), (1,)), ((), ())...]
    convert_element_type x18 -> x2, other arithmetic: 36.7 us -> 2.98 us  [the longest x1 2.96 us: total(): return lax.psum(share, 'frame').astype(f32)]
  transfers between devices with their start and end apart: 9 -> 6, of which waited for: 8 -> 5; matrix products, arithmetic and copies ran while one was open for 14% -> 16% of each run, Pallas kernels for 0% -> 0%
where the time goes in v1:
time: 570 us; the launch traced here: 562 us
  waiting for transfers between devices  251 us (44%)
  Pallas kernels  124 us (22%)
  local copies, waits for them, and re-layouts  95.5 us (17%)
  blocking collectives  55.6 us (10%)
  between operations  15.1 us (3%)
  matrix products  14.6 us (3%)
  other arithmetic  5.94 us (1%)
    psum x1, waiting for transfers between devices, total(): return lax.psum(share, 'frame').astype(f32)  92.7 us
    unnamed x8, waiting for transfers between devices  75.6 us
    reduce_scatter x1, waiting for transfers between devices, total(): share = lax.psum_scatter(value, 'video', scatter_dimension=0, tiled=True)  57.7 us
    pallas_call x1, Pallas kernels, call_k2(): pl.pallas_call(functools.partial(k2, MB), grid=(6,), in_specs=specs, out_...  51.2 us
    pallas_call x1, Pallas kernels, call_k3(): pl.pallas_call(k3, grid=(6,), in_specs=specs, out_specs=[full(RR, D), blk...  42.1 us
    psum x1, blocking collectives, local(): vector = lax.psum(vector, ('video', 'frame'))  40 us
    pallas_call x1, Pallas kernels, call_k1(): pl.pallas_call(k1, grid=(6,), in_specs=specs, out_specs=[blk(RP, 384), bl...  30.7 us
    unnamed x51, local copies, waits for them, and re-layouts  27.5 us
  transfers between devices with their start and end apart: 6, of which 5 were waited for; matrix products, arithmetic and copies ran while one was open for 16% of the time, Pallas kernels for 0%

profile of v1, /device:TPU:0, one launch (start us, length us, event | category | flops | bytes accessed | tf_op | source)
XLA Modules:
  0.0 561.5 jit_solution(4439581176865921824)
XLA Ops:
  9.6 15.6 %all-gather = bf16[6,6144]{1,0:T(8,128)(2,1)S(1)} all-gather(bf16[6,768]{1,0:T(8,128)(2,1)S(1)} %get-tuple-element.168), channel_id=2, replica_groups=mesh['frame'=8,'video'=4] {'frame'}, dimensions={1}, use_global_device_ids=true | all-gather | bytes 82944 | tf_op jit(solution)/shard_map/all_gather | solution.py:281
  35.7 30.7 %shard_map.322 = (bf16[6,1280,384]{2,1,0:T(8,128)(2,1)}, bf16[6,12,208,208]{3,2,1,0:T(8,128)(2,1)}, bf16[1280,768]{1,0:T(8,128)(2,1)}, bf16[6,1280,128]{2,1,0:T(8,128)(2,1)}, f32[1248,768]{1,0:T(8,128)}) custom-call(bf16[6,1,197,768]{3,2,1,0:T(8,128)(2,1)} %vid.3, f32[6,768]{1,0:T(8,128)} %convolution_add_fusion.mnext, bf16[768,2304]{1,0:T(8,128)(2,1)} %wv.3, ...), custom_call_target="tpu_custom_call" | custom-call | tf_op jit(solution)/shard_map/pallas_call | solution.py:139
  66.3 51.2 %shard_map.323 = (bf16[6,1,198,768]{3,2,1,0:T(8,128)(2,1)}, f32[1248,768]{1,0:T(8,128)}, bf16[6,768,512]{2,1,0:T(8,128)(2,1)}, bf16[6,768,512]{2,1,0:T(8,128)(2,...) custom-call(f32[1248,768]{1,0:T(8,128)} %get-tuple-element.32.mid, bf16[6,1,198,768]{3,2,1,0:T(8,128)(2,1)} %cot.1, s32[6]{0:T(128)} %live.1, ...), custom_call_target="tpu_custom_call" | custom-call | tf_op jit(solution)/shard_map/pallas_call | solution.py:80
  117.5 42.1 %shard_map.324 = (f32[1248,768]{1,0:T(8,128)}, bf16[6,768,512]{2,1,0:T(8,128)(2,1)}, f32[8,768]{1,0:T(8,128)}) custom-call(bf16[6,1,197,768]{3,2,1,0:T(8,128)(2,1)} %vid.3, f32[6,768]{1,0:T(8,128)} %convolution_add_fusion.mnext, f32[1248,768]{1,0:T(8,128)} %get-tuple-element.34.gmid, bf16[6,1280,384]{2,1,0:T(8,128)(2,1)} %get-tuple-element.35.qkv, ...), custom_call_target="tpu_custom_call" | custom-call | tf_op jit(solution)/shard_map/pallas_call | solution.py:204
  163.2 7.7 %reshape.374 = bf16[6,768,4,128]{3,2,1,0:T(4,128)(2,1)} reshape(bf16[6,768,512]{2,1,0:T(8,128)(2,1)} %get-tuple-element.43) | data formatting | bytes 9437184 | tf_op jit(solution)/shard_map/reshape | solution.py:366
  170.9 8.4 %copy.109 = bf16[6,768,4,128]{1,3,0,2:T(8,128)(2,1)} copy(bf16[6,768,4,128]{3,2,1,0:T(4,128)(2,1)} %reshape.374) | data formatting | bytes 9437184 | tf_op jit(solution)/shard_map/reshape | solution.py:366
  179.3 6.6 %copy.126 = bf16[768,3072]{1,0:T(8,128)(2,1)} copy(bf16[768,3072]{0,1:T(8,128)(2,1)} %bitcast.140) | data formatting | bytes 9437184
  186.0 7.8 %reshape.376 = bf16[6,768,4,128]{3,2,1,0:T(4,128)(2,1)} reshape(bf16[6,768,512]{2,1,0:T(8,128)(2,1)} %get-tuple-element.44) | data formatting | bytes 9437184 | tf_op jit(solution)/shard_map/reshape | solution.py:364
  193.8 8.4 %copy.110 = bf16[6,768,4,128]{1,3,0,2:T(8,128)(2,1)} copy(bf16[6,768,4,128]{3,2,1,0:T(4,128)(2,1)} %reshape.376) | data formatting | bytes 9437184 | tf_op jit(solution)/shard_map/reshape | solution.py:364
  202.3 7.0 %copy.128 = bf16[768,3072]{1,0:T(8,128)(2,1)} copy(bf16[768,3072]{0,1:T(8,128)(2,1)} %bitcast.141) | data formatting | bytes 9437184
  209.3 7.9 %reshape.378 = bf16[6,768,4,128]{3,2,1,0:T(4,128)(2,1)} reshape(bf16[6,768,512]{2,1,0:T(8,128)(2,1)} %get-tuple-element.45) | data formatting | bytes 9437184 | tf_op jit(solution)/shard_map/reshape | solution.py:365
  217.2 8.6 %copy.111 = bf16[4,6,128,768]{3,2,1,0:T(8,128)(2,1)} copy(bf16[4,6,128,768]{2,0,3,1:T(4,128)(2,1)} %bitcast.142) | data formatting | bytes 9437184 | tf_op jit(solution)/shard_map/transpose | solution.py:365
  226.6 3.2 fusion.55
  230.9 2.5 slice.105
  235.6 17.6 %reduce-scatter.13.cloned.1.call-done = bf16[192,3072]{1,0:T(8,128)(2,1)} async-done(((bf16[768,3072]{1,0:T(8,128)(2,1)}), bf16[192,3072]{1,0:T(8,128)(2,1)}) %reduce-scatter.13.cloned.1.call-update) | async-done | bytes 1179664
  253.2 2.5 copy.127
  255.7 57.9 %reduce-scatter.15.cloned.1.call-done = bf16[192,3072]{1,0:T(8,128)(2,1)} async-done(((bf16[768,3072]{1,0:T(8,128)(2,1)}), bf16[192,3072]{1,0:T(8,128)(2,1)}) %reduce-scatter.15.cloned.1.call-update) | async-done | bytes 1179664
  313.6 2.5 copy.129
  316.1 57.7 %reduce-scatter.11.cloned.1.call-done = bf16[768,768]{1,0:T(8,128)(2,1)} async-done(((bf16[3072,768]{1,0:T(8,128)(2,1)}), bf16[768,768]{1,0:T(8,128)(2,1)}) %reduce-scatter.11.cloned.1.call-update) | async-done | bytes 1179664 | tf_op jit(solution)/shard_map/reduce_scatter | solution.py:361
  373.9 40.0 %psum.28 = f32[9216]{0:T(1024)S(1)} all-reduce(f32[9216]{0:T(1024)S(1)} %constant_dynamic-update-slice_fusion.14), channel_id=1, replica_groups=mesh['frame'=8,'video'=4] {'video','frame'}, use_global_device_ids=true, to_apply=%region_13.0 | all-reduce | flops 9216 | bytes 73728 | tf_op jit(solution)/shard_map/psum | solution.py:381
  417.0 24.6 %all-gather.4.cloned.1.call-done = bf16[192,1,6144]{2,1,0:T(2,128)(2,1)} async-done(((bf16[6,1,6144]{2,1,0:T(2,128)(2,1)}), bf16[192,1,6144]{2,1,0:T(2,128)(2,1)}) %all-gather.4.cloned.1.call-update) | async-done | bytes 2359312 | tf_op jit(solution)/shard_map/all_gather | solution.py:388
  441.6 3.7 copy.180
  451.2 92.7 %all-reduce.3.cloned.1.call-done = (bf16[192,3072]{0,1:T(8,128)(2,1)}, bf16[192,3072]{0,1:T(8,128)(2,1)}, bf16[768,768]{1,0:T(8,128)(2,1)}) async-done(((bf16[192,3072]{0,1:T(8,128)(2,1)}, bf16[192,3072]{0,1:T(8,128)(2,1)}, bf16[768,768]{1,0:T(8,128)(2,1)}), (bf16[192,3072]{0,1:T(8,128)(2,1)}, bf16[192,3072]{0,1:T(8,128)(2,1)}, bf16[768,768]{1,0:T(8,128)(2,1)})) %all-reduce.3.cloned.1.call-update) | async-done | bytes 3538960 | tf_op jit(solution)/shard_map/psum | solution.py:362
  548.4 3.0 convert_element_type.144
  (136 shorter events, 36.5 us)
Async XLA Ops:
  7.2 1.3 copy-start
  7.2 20.4 %copy-start.6 = (f32[768]{0:T(1024)S(1)}, f32[768]{0:T(1024)}, u32[]{:S(2)}) copy-start(f32[768]{0:T(1024)} %param.24) | copy-start | bytes 9220
  7.2 20.4 %copy-start.7 = (f32[768]{0:T(1024)S(1)}, f32[768]{0:T(1024)}, u32[]{:S(2)}) copy-start(f32[768]{0:T(1024)} %param.25) | copy-start | bytes 9220
  7.2 219.4 %reduce-scatter.9.cloned.1.call-start = ((), (), s32[]{:S(2)}) async-start(), calls=%async_computation.4 | async-start | bytes 221184 | tf_op jit(solution)/shard_map/reduce_scatter | solution.py:303
  27.5 3.7 copy-start.10
  27.5 4.3 copy-start.11
  27.5 4.9 copy-start.8
  27.5 5.5 copy-start.12
  27.6 6.0 %copy-start.13 = (f32[768]{0:T(1024)S(1)}, f32[768]{0:T(1024)}, u32[]{:S(2)}) copy-start(f32[768]{0:T(1024)} %param.32) | copy-start | bytes 9220
  27.6 6.6 %copy-start.14 = (f32[768]{0:T(1024)S(1)}, f32[768]{0:T(1024)}, u32[]{:S(2)}) copy-start(f32[768]{0:T(1024)} %param.33) | copy-start | bytes 9220
  27.6 7.2 %copy-start.2 = (bf16[768,768]{1,0:T(8,128)(2,1)S(1)}, bf16[768,768]{1,0:T(8,128)(2,1)}, u32[]{:S(2)}) copy-start(bf16[768,768]{1,0:T(8,128)(2,1)} %param.27) | copy-start | bytes 3538948
  163.1 90.0 %reduce-scatter.13.cloned.1.call-start = ((), (), s32[]{:S(2)}) async-start(), calls=%async_computation.7 | async-start | bytes 5898240
  186.0 127.6 %reduce-scatter.15.cloned.1.call-start = ((), (), s32[]{:S(2)}) async-start(), calls=%async_computation.8 | async-start | bytes 5898240
  209.3 164.5 %reduce-scatter.11.cloned.1.call-start = ((), (), s32[]{:S(2)}) async-start(), calls=%async_computation.5 | async-start | bytes 5898240 | tf_op jit(solution)/shard_map/reduce_scatter | solution.py:361
  225.9 215.7 %all-gather.4.cloned.1.call-start = ((), (), s32[]{:S(2)}) async-start(), calls=%async_computation.6 | async-start | bytes 4866048 | tf_op jit(solution)/shard_map/all_gather | solution.py:388
  226.6 3.4 copy-start.5
  229.9 3.5 copy-start.9
  230.8 313.1 %all-reduce.3.cloned.1.call-start = ((), (), s32[]{:S(2)}) async-start(), calls=%async_computation.9 | async-start | bytes 8650752 | tf_op jit(solution)/shard_map/psum | solution.py:362
  543.9 1.8 copy-start.1
  548.4 3.0 copy-start.4
  551.4 1.8 copy-start.3
Sparse Core Ops, SparseCore 0:
  163.3 31.2 reduce-scatter.8
  197.9 55.2 reduce-scatter.12
  256.5 57.0 reduce-scatter.14
  316.7 57.0 reduce-scatter.10
  377.7 63.8 all-gather.3
  445.4 98.5 all-reduce.2
